TPU v7x, 32 devices: a whole 2x2x4 slice. The times are simulated.
32 devices in a mesh: groups: 2 (over x), node: 8 (over z, y), local: 2 (over core).
Axes of the slice: x: 2, y: 2, z: 4, core: 2. Of those that a mesh axis runs over, the one named last changes fastest.
Arguments:
- tokens: bfloat16 [4096, 3584], P(('groups', 'node', 'local')), parts along dimension 0, may hold values from -6 to 6
- expert_ids: int32 [4096, 8], P(('groups', 'node', 'local')), parts along dimension 0, may hold values from 0 to 15, as said below
- gate_levels: int32 [4096, 8], P(('groups', 'node', 'local')), parts along dimension 0, may hold values from 1 to 255
- placement: int32 [16], replicated, may hold values from 0 to 15, each once
- w_gate: bfloat16 [16, 3584, 1024], P(('node', 'local')), may hold values from -0.09375 to 0.09375
- w_up: bfloat16 [16, 3584, 1024], P(('node', 'local')), may hold values from -0.09375 to 0.09375
- w_down: bfloat16 [16, 1024, 3584], P(('node', 'local')), may hold values from -0.1875 to 0.1875
Outputs:
- mixed: bfloat16 [4096, 3584], P(('groups', 'node', 'local')), parts along dimension 0
There are 2 independent parts, one for each index of `groups`. A program takes and returns all parts, laid end to end along the dimension named above; an argument that names none is the same for every part. Nothing has to cross between parts.
Inputs may be any that keep to these rules, and one draw needn't show every extreme that they name: `expert_ids`: each row names 8 different experts. In each aligned block of 128 rows (the rows of one device) every expert is named by at least 48 and at most 80 rows, and one expert, the same in every block of a part, by exactly 80 rows. `placement`: each device of a part holds exactly one expert.
All inputs are finite; a program needn't handle non-finite values.
Results may differ from a plain program's by a relative error of at most 0.0059.
Values may be sent and summed in bfloat16 or wider, within the bound.
A program may use at most 128 MiB of HBM per device.

v0:
```python
import jax
import jax.numpy as jnp
from jax import lax
from jax.sharding import PartitionSpec as P

route_scale = 2.5


def device_shares(expert_ids, gate_levels, placement):
    device_count = placement.shape[0]
    levels = gate_levels.astype(jnp.float32)
    shares = route_scale * levels / jnp.sum(levels, axis=1, keepdims=True)
    expert_iota = lax.broadcasted_iota(jnp.int32, (1, 1, device_count), 2)
    target = jnp.sum(
        jnp.where(expert_ids[:, :, None] == expert_iota, placement[None, None, :], 0), axis=2
    )
    return jnp.sum(
        jnp.where(target[:, :, None] == expert_iota, shares[:, :, None], 0.0), axis=1
    )


def local(tokens, expert_ids, gate_levels, placement, w_gate, w_up, w_down):
    weight = device_shares(expert_ids, gate_levels, placement)
    me = lax.axis_index("node") * lax.axis_size("local") + lax.axis_index("local")
    rows = lax.all_gather(tokens, ("node", "local"), axis=0, tiled=True)
    weights = lax.all_gather(weight, ("node", "local"), axis=0, tiled=True)
    mine = lax.dynamic_slice_in_dim(weights, me, 1, axis=1)
    gate_act = jnp.dot(rows, w_gate[0], preferred_element_type=jnp.float32)
    up_act = jnp.dot(rows, w_up[0], preferred_element_type=jnp.float32)
    hidden_act = (jax.nn.silu(gate_act) * up_act).astype(jnp.bfloat16)
    out = jnp.dot(hidden_act, w_down[0], preferred_element_type=jnp.float32)
    part = (out * mine).astype(jnp.bfloat16)
    return lax.psum_scatter(part, ("node", "local"), scatter_dimension=0, tiled=True)


def solution(mesh):
    in_specs = (
        P(("groups", "node", "local"), None),
        P(("groups", "node", "local"), None),
        P(("groups", "node", "local"), None),
        P(),
        P(("node", "local"), None, None),
        P(("node", "local"), None, None),
        P(("node", "local"), None, None),
    )
    out_specs = P(("groups", "node", "local"), None)
    return jax.shard_map(local, mesh=mesh, in_specs=in_specs, out_specs=out_specs, check_vma=False)
```

profile of v0, /device:TPU:0, one launch (start us, length us, event | category | flops | bytes accessed | tf_op | source)
XLA Modules:
  0.0 344.4 jit_solution(9161354420114053575)
XLA Ops:
  6.5 0.0 all-gather.2.cloned.1.call-start
  6.5 0.7 all-gather.2.cloned.1.call-update
  7.3 0.0 reduce-scatter.2.cloned.1.call-start
  7.3 0.7 convert_reduce_fusion
  8.0 0.8 select_reduce_fusion.1
  8.8 0.7 multiply_divide_fusion
  9.5 24.0 %all_gather.7 = f32[2048,16]{0,1:T(8,128)S(1)} all-gather(f32[128,16]{0,1:T(8,128)S(1)} %select_reduce_fusion), channel_id=1, replica_groups=mesh['groups'=2,'node'=8,'local'=2] {'node','local'}, dimensions={0}, use_global_device_ids=true | all-gather | bytes 139264 | tf_op jit(solution)/shard_map/all_gather | solution.py:26
  33.5 92.9 %all-gather.2.cloned.1.call-done = bf16[2048,3584]{1,0:T(8,128)(2,1)} async-done(((bf16[128,3584]{1,0:T(8,128)(2,1)}), bf16[2048,3584]{1,0:T(8,128)(2,1)}) %all-gather.2.cloned.1.call-update) | async-done | bytes 14680080 | tf_op jit(solution)/shard_map/all_gather | solution.py:25
  126.4 0.0 copy-start
  126.4 0.0 slice-start
  126.4 21.5 %fusion.1 = f32[2048,1024]{1,0:T(8,128)} fusion(bf16[2048,3584]{1,0:T(8,128)(2,1)} %all-gather.2.cloned.1.call-done, bf16[1,3584,1024]{2,1,0:T(8,128)(2,1)} %param.12), kind=kOutput, calls=%fused_computation.3 | convolution fusion | flops 15032385536 | bytes 30408704 | tf_op jit(solution)/shard_map/dot_general | solution.py:29
  147.9 0.0 copy-done
  147.9 0.0 slice-start.1
  147.9 20.8 %multiply_convert_fusion.1 = bf16[2048,1024]{1,0:T(8,128)(2,1)} fusion(f32[2048,1024]{1,0:T(8,128)} %fusion.1, bf16[2048,3584]{1,0:T(8,128)(2,1)S(1)} %copy-done, bf16[1,3584,1024]{2,1,0:T(8,128)(2,1)} %param.11), kind=kOutput, calls=%fused_computation.1 | convolution fusion | flops 15044968448 | bytes 34603008 | tf_op jit(solution)/shard_map/dot_general | solution.py:28
  168.7 0.0 slice-done
  168.7 0.0 slice-done.1
  168.7 20.9 %multiply_convert_fusion = bf16[2048,3584]{1,0:T(8,128)(2,1)} fusion(bf16[2048,1024]{1,0:T(8,128)(2,1)} %multiply_convert_fusion.1, f32[2048]{0:T(1024)S(1)} %bitcast.15, bf16[1,1024,3584]{2,1,0:T(8,128)(2,1)S(1)} %bitcast.17), kind=kOutput, calls=%fused_computation | convolution fusion | flops 15047065600 | bytes 26222592 | tf_op jit(solution)/shard_map/dot_general | solution.py:31
  189.6 0.0 reduce-scatter.2.cloned.1.call-update
  189.6 148.0 %reduce-scatter.2.cloned.1.call-done = bf16[128,3584]{1,0:T(8,128)(2,1)} async-done(((bf16[2048,3584]{1,0:T(8,128)(2,1)}), bf16[128,3584]{1,0:T(8,128)(2,1)}) %reduce-scatter.2.cloned.1.call-update) | async-done | bytes 917520 | tf_op jit(solution)/shard_map/reduce_scatter | solution.py:33
  (3 shorter events, 0.0 us)
Async XLA Ops:
  6.5 119.8 %all-gather.2.cloned.1.call-start = ((), (), s32[]{:S(2)}) async-start(), calls=%async_computation.1 | async-start | bytes 15597568 | tf_op jit(solution)/shard_map/all_gather | solution.py:25
  7.3 330.3 %reduce-scatter.2.cloned.1.call-start = ((), (), s32[]{:S(2)}) async-start(), calls=%async_computation.2 | async-start | bytes 15597568 | tf_op jit(solution)/shard_map/reduce_scatter | solution.py:33
  126.4 21.5 %copy-start = (bf16[2048,3584]{1,0:T(8,128)(2,1)S(1)}, bf16[2048,3584]{1,0:T(8,128)(2,1)}, u32[]{:S(2)}) copy-start(bf16[2048,3584]{1,0:T(8,128)(2,1)} %all-gather.2.cloned.1.call-done) | copy-start | bytes 44040196
  126.4 42.3 %slice-start = ((s8[7340032]{0:T(1024)(128)(4,1)}), s8[4194304]{0:T(1024)(128)(4,1)S(1)}, s32[]{:S(2)}) async-start(s8[7340032]{0:T(1024)(128)(4,1)} %bitcast.16), calls=%async_computation.3 | async-start | bytes 8388608
  147.9 20.8 %slice-start.1 = ((s8[7340032]{0:T(1024)(128)(4,1)}), s8[3145728]{0:T(1024)(128)(4,1)S(1)}, s32[]{:S(2)}) async-start(s8[7340032]{0:T(1024)(128)(4,1)} %bitcast.16), calls=%async_computation.4 | async-start | bytes 6291456
Sparse Core Ops, SparseCore 0:
  9.7 116.6 all-gather.1
  189.7 147.7 reduce-scatter.1
where the time goes:
time: 345 us; the launch traced here: 344 us
  waiting for transfers between devices  242 us (70%)
  matrix products  63.2 us (18%)
  blocking collectives  24 us (7%)
  between operations  13.4 us (4%)
    reduce_scatter x1, waiting for transfers between devices, local(): lax.psum_scatter(part, ('node', 'local'), scatter_dimension=0, tiled=True)  148 us
    all_gather x1, waiting for transfers between devices, local(): rows = lax.all_gather(tokens, ('node', 'local'), axis=0, tiled=True)  92.9 us
    all_gather x1, blocking collectives, local(): weights = lax.all_gather(weight, ('node', 'local'), axis=0, tiled=True)  24 us
    dot_general x1, matrix products, local(): up_act = jnp.dot(rows, w_up[0], preferred_element_type=jnp.float32)  21.5 us
    dot_general x1, matrix products, local(): out = jnp.dot(hidden_act, w_down[0], preferred_element_type=jnp.float32)  20.9 us
    dot_general x1, matrix products, local(): gate_act = jnp.dot(rows, w_gate[0], preferred_element_type=jnp.float32)  20.8 us
  transfers between devices with their start and end apart: 2, of which 2 were waited for; matrix products, arithmetic and copies ran while one was open for 1% of the time, Pallas kernels for 0%

commit v1 on v0

--- a/solution.py
+++ b/solution.py
@@ -1,9 +1,16 @@
+import functools
+
 import jax
 import jax.numpy as jnp
 from jax import lax
+from jax.experimental import pallas as pl
+from jax.experimental.pallas import tpu as pltpu
 from jax.sharding import PartitionSpec as P
 
+MESH = pl.DeviceIdType.MESH
 route_scale = 2.5
+LANES = 128
+VMEM_LIMIT = 64 * 1024 * 1024 - 256 * 1024
 
 
 def device_shares(expert_ids, gate_levels, placement):
@@ -19,7 +26,7 @@
     )
 
 
-def local(tokens, expert_ids, gate_levels, placement, w_gate, w_up, w_down):
+def gathered(tokens, expert_ids, gate_levels, placement, w_gate, w_up, w_down):
     weight = device_shares(expert_ids, gate_levels, placement)
     me = lax.axis_index("node") * lax.axis_size("local") + lax.axis_index("local")
     rows = lax.all_gather(tokens, ("node", "local"), axis=0, tiled=True)
@@ -33,7 +40,318 @@
     return lax.psum_scatter(part, ("node", "local"), scatter_dimension=0, tiled=True)
 
 
+def kernel(
+    n,
+    columns,
+    x_hbm,
+    wg_hbm,
+    wu_hbm,
+    wd_hbm,
+    out_ref,
+    xbuf,
+    wg,
+    wu,
+    wd,
+    mine,
+    sib,
+    rbuf,
+    stage,
+    hid,
+    load_sem,
+    ag_send,
+    ag_recv,
+    xs_send,
+    xs_recv,
+    ys_send,
+    ys_recv,
+    rs_send,
+    rs_recv,
+):
+    node = lax.axis_index("node")
+    core = lax.axis_index("local")
+    K = n // 2
+    T = x_hbm.shape[0]
+    H = T // 2
+    Q = H // 2
+    D = wg.shape[0]
+    F = wg.shape[1]
+    if columns == 2:
+        side = node % 2
+        level = node // 2
+        pos = (1 - side) * level + side * (n - 1 - level)
+
+        def node_at(p):
+            far = p // K
+            return (1 - far) * (2 * p) + far * (2 * (n - 1 - p) + 1)
+    else:
+        pos = node
+
+        def node_at(p):
+            return p
+
+    right = {"node": node_at((pos + 1) % n), "local": core}
+    left = {"node": node_at((pos + n - 1) % n), "local": core}
+    other = {"node": node, "local": 1 - core}
+
+    loads = [pltpu.make_async_copy(x_hbm.at[pl.ds(h * H, H)], xbuf.at[pl.ds(h * n * T, H)], load_sem.at[h]) for h in range(2)]
+    loads += [
+        pltpu.make_async_copy(src, dst, load_sem.at[2 + i])
+        for i, (src, dst) in enumerate(((wg_hbm, wg), (wu_hbm, wu), (wd_hbm, wd)))
+    ]
+    for copy in loads:
+        copy.start()
+
+    barrier = pltpu.get_barrier_semaphore()
+    for device in (left, right, other):
+        pl.semaphore_signal(barrier, inc=1, device_id=device, device_id_type=MESH)
+    pl.semaphore_wait(barrier, 3)
+
+    def count(s):
+        return 1 if s in (0, K) else 2
+
+    def xbase(h, s):
+        return h * n * T + (0 if s == 0 else T + (s - 1) * 2 * T)
+
+    def mbase(h, s):
+        return h * n * H + (0 if s == 0 else H + (s - 1) * T)
+
+    def ag(d, h, s, sub):
+        if s == 1:
+            src = xbase(h, 0) + sub * Q
+        else:
+            src = xbase(h, s - 1) + d * H + sub * Q
+        if s < K:
+            dst = xbase(h, s) + d * H + sub * Q
+        else:
+            dst = xbase(h, s) + sub * Q
+        i = ((d * 2 + h) * K + s - 1) * 2 + sub
+        return pltpu.make_async_remote_copy(
+            xbuf.at[pl.ds(src, Q)],
+            xbuf.at[pl.ds(dst, Q)],
+            ag_send.at[i],
+            ag_recv.at[i],
+            device_id=(right, left)[d],
+            device_id_type=MESH,
+        )
+
+    def xs(h, s):
+        size = count(s) * H
+        i = h * (K + 1) + s
+        return pltpu.make_async_remote_copy(
+            xbuf.at[pl.ds(xbase(h, s), size)],
+            xbuf.at[pl.ds(xbase(h, s) + size, size)],
+            xs_send.at[i],
+            xs_recv.at[i],
+            device_id=other,
+            device_id_type=MESH,
+        )
+
+    order = [(0, s) for s in range(K + 1)] + [(1, s) for s in range(K + 1)]
+
+    def ys(h, s):
+        size = count(s) * H
+        i = h * (K + 1) + s
+        return pltpu.make_async_remote_copy(
+            stage.at[order.index((h, s)) % 2, pl.ds(0, size)],
+            sib.at[pl.ds(mbase(h, s), size)],
+            ys_send.at[i],
+            ys_recv.at[i],
+            device_id=other,
+            device_id_type=MESH,
+        )
+
+    def mrow(d, h, s, sub):
+        return mbase(h, s) + (d * H if s < K else 0) + sub * Q
+
+    def rrow(d, h, s, sub):
+        return h * (n - 1) * H + ((s - 1) * 2 + (d if s < K else 0)) * H + sub * Q
+
+    def rs(d, h, s, sub):
+        i = ((d * 2 + h) * K + s - 1) * 2 + sub
+        return pltpu.make_async_remote_copy(
+            mine.at[pl.ds(mrow(d, h, s, sub), Q)],
+            rbuf.at[pl.ds(rrow(d, h, s, sub), Q)],
+            rs_send.at[i],
+            rs_recv.at[i],
+            device_id=(left, right)[d],
+            device_id_type=MESH,
+        )
+
+    def messages(s):
+        return [(d, sub) for sub in range(2) for d in range(2) if s < K or sub == d]
+
+    def arrive(h, s):
+        for d, sub in ([(0, 0), (0, 1)] if s == 0 else messages(s)):
+            if s > 0:
+                ag(d, h, s, sub).wait_recv()
+                if s < K and (d, sub) in messages(s + 1):
+                    ag(d, h, s + 1, sub).start()
+            else:
+                for way, part in messages(1):
+                    if part == sub:
+                        ag(way, h, 1, sub).start()
+        xs(h, s).start()
+
+    me = node * 2 + core
+
+    def compute(h, s):
+        size = count(s) * H
+        rows = 2 * size
+        xs(h, s).wait_recv()
+        base = xbase(h, s)
+        place = order.index((h, s))
+        if place >= 2:
+            ys(*order[place - 2]).wait_send()
+        lanes = lax.broadcasted_iota(jnp.int32, (rows, LANES), 1)
+        marks = xbuf[base : base + rows, D : D + LANES].astype(jnp.float32)
+        share = jnp.sum(
+            jnp.where((lanes == me) | (lanes == me + LANES // 2), marks, 0.0), axis=1, keepdims=True
+        )
+        wide = 256
+
+        @pl.loop(0, F // wide)
+        def _(f):
+            cols = pl.ds(pl.multiple_of(f * wide, wide), wide)
+            x = xbuf[base : base + rows, 0:D]
+            gate = jnp.dot(x, wg[:, cols], preferred_element_type=jnp.float32)
+            up = jnp.dot(x, wu[:, cols], preferred_element_type=jnp.float32)
+            hid[0:rows, cols] = (gate / (1.0 + jnp.exp(-gate)) * up).astype(jnp.bfloat16)
+
+        tile = 512 if D % 512 == 0 else 256
+
+        @pl.loop(0, D // tile)
+        def _(f):
+            cols = pl.ds(pl.multiple_of(f * tile, tile), tile)
+            res = jnp.dot(hid[0:rows, :], wd[:, cols], preferred_element_type=jnp.float32)
+            res = (res * share).astype(jnp.bfloat16)
+            mine[mbase(h, s) : mbase(h, s) + size, cols] = res[0:size]
+            stage[place % 2, 0:size, cols] = res[size:rows]
+
+        ys(h, s).start()
+
+    def reduce(h, s):
+        ys(h, s).wait_recv()
+        for d, sub in messages(s):
+            m = mrow(d, h, s, sub)
+            more = s < K and (d, sub) in messages(s + 1)
+            if more:
+                rs(d, h, s + 1, sub).wait_recv()
+            r = rrow(d, h, s + 1, sub) if more else 0
+
+            for a in range(0, Q, 16):
+                total = mine[m + a : m + a + 16, :].astype(jnp.float32) + sib[m + a : m + a + 16, :].astype(jnp.float32)
+                if more:
+                    total = total + rbuf[r + a : r + a + 16, :].astype(jnp.float32)
+                mine[m + a : m + a + 16, :] = total.astype(jnp.bfloat16)
+            rs(d, h, s, sub).start()
+
+    def finish(h):
+        ys(h, 0).wait_recv()
+        for sub in range(2):
+            m = mbase(h, 0) + sub * Q
+            for d in range(2):
+                rs(d, h, 1, sub).wait_recv()
+            r0, r1 = rrow(0, h, 1, sub), rrow(1, h, 1, sub)
+            for a in range(0, Q, 16):
+                total = mine[m + a : m + a + 16, :].astype(jnp.float32) + sib[m + a : m + a + 16, :].astype(jnp.float32)
+                total = total + rbuf[r0 + a : r0 + a + 16, :].astype(jnp.float32)
+                total = total + rbuf[r1 + a : r1 + a + 16, :].astype(jnp.float32)
+                o = h * H + sub * Q + a
+                out_ref[o : o + 16, :] = total.astype(jnp.bfloat16)
+
+    loads[0].wait()
+    arrive(0, 0)
+    loads[1].wait()
+    for copy in loads[2:]:
+        copy.wait()
+    for s in range(1, K + 1):
+        arrive(0, s)
+        if s == K - 1:
+            arrive(1, 0)
+        compute(0, s - 1)
+    arrive(1, 1)
+    compute(0, K)
+    compute(1, 0)
+    todo = [(0, s) for s in range(K, 0, -1)]
+    for s in range(2, K + 1):
+        arrive(1, s)
+        if s >= K - 1:
+            reduce(*todo.pop(0))
+        compute(1, s - 1)
+    reduce(*todo.pop(0))
+    compute(1, K)
+    for item in todo:
+        reduce(*item)
+    reduce(1, K)
+    finish(0)
+    for s in range(K - 1, 0, -1):
+        reduce(1, s)
+    finish(1)
+
+    for h in range(2):
+        for s in range(1, K + 1):
+            for d, sub in messages(s):
+                ag(d, h, s, sub).wait_send()
+                rs(d, h, s, sub).wait_send()
+        for s in range(K + 1):
+            xs(h, s).wait_send()
+    for item in order[-2:]:
+        ys(*item).wait_send()
+
+
+def ring(n, columns, tokens, expert_ids, gate_levels, placement, w_gate, w_up, w_down):
+    T, D = tokens.shape
+    F = w_gate.shape[2]
+    K = n // 2
+    weight = device_shares(expert_ids, gate_levels, placement)
+    high = lax.reduce_precision(weight, 8, 7)
+    low = weight - high
+    room = ((0, 0), (0, LANES // 2 - placement.shape[0]))
+    rows = jnp.concatenate(
+        [tokens, jnp.pad(high, room).astype(jnp.bfloat16), jnp.pad(low, room).astype(jnp.bfloat16)],
+        axis=1,
+    )
+    bf = jnp.bfloat16
+    dma = pltpu.SemaphoreType.DMA
+    return pl.pallas_call(
+        functools.partial(kernel, n, columns),
+        out_shape=jax.ShapeDtypeStruct((T, D), bf),
+        in_specs=[pl.BlockSpec(memory_space=pl.ANY)] * 4,
+        out_specs=pl.BlockSpec(memory_space=pltpu.VMEM),
+        scratch_shapes=[
+            pltpu.VMEM((2 * n * T, D + LANES), bf),
+            pltpu.VMEM((D, F), bf),
+            pltpu.VMEM((D, F), bf),
+            pltpu.VMEM((F, D), bf),
+            pltpu.VMEM((n * T, D), bf),
+            pltpu.VMEM((n * T, D), bf),
+            pltpu.VMEM(((n - 1) * T, D), bf),
+            pltpu.VMEM((2, T, D), bf),
+            pltpu.VMEM((2 * T, F), bf),
+            dma((5,)),
+            dma((8 * K,)),
+            dma((8 * K,)),
+            dma((2 * K + 2,)),
+            dma((2 * K + 2,)),
+            dma((2 * K + 2,)),
+            dma((2 * K + 2,)),
+            dma((8 * K,)),
+            dma((8 * K,)),
+        ],
+        compiler_params=pltpu.CompilerParams(
+            collective_id=0, has_side_effects=True, vmem_limit_bytes=VMEM_LIMIT
+        ),
+        cost_estimate=pl.CostEstimate(
+            flops=12 * n * T * D * F, bytes_accessed=6 * D * F, transcendentals=2 * n * T * F
+        ),
+    )(rows, w_gate[0], w_up[0], w_down[0])
+
+
 def solution(mesh):
+    nodes = mesh.shape["node"]
+    ringed = 4 <= nodes <= 8 and nodes % 2 == 0 and mesh.shape["local"] == 2
+    columns = 2 if mesh.shape["groups"] == 2 else 1
+    body = functools.partial(ring, nodes, columns) if ringed else gathered
     in_specs = (
         P(("groups", "node", "local"), None),
         P(("groups", "node", "local"), None),
@@ -44,4 +362,4 @@
         P(("node", "local"), None, None),
     )
     out_specs = P(("groups", "node", "local"), None)
-    return jax.shard_map(local, mesh=mesh, in_specs=in_specs, out_specs=out_specs, check_vma=False)
+    return jax.shard_map(body, mesh=mesh, in_specs=in_specs, out_specs=out_specs, check_vma=False)

time: 345 us -> 158 us (0.46)
  waiting for transfers between devices: 242 us -> 0 us
  Pallas kernels: 0 us -> 151 us
  matrix products: 63.2 us -> 0 us
  blocking collectives: 24 us -> 0 us
  between operations: 13.4 us -> 0.05 us
  local copies, waits for them, and re-layouts: 0.02 us -> 4.43 us
    pallas_call x0 -> x1, Pallas kernels: none -> 151 us  [ring(): pl.pallas_call(functools.partial(kernel, n, columns), out_shape=jax.Shape...]
    reduce_scatter x1 -> x0, waiting for transfers between devices: 148 us -> none  [local(): lax.psum_scatter(part, ('node', 'local'), scatter_dimension=0, tiled=True)]
    all_gather x1 -> x0, waiting for transfers between devices: 92.9 us -> none  [local(): rows = lax.all_gather(tokens, ('node', 'local'), axis=0, tiled=True)]
    dot_general x3 -> x0, matrix products: 63.2 us -> none  [the longest x1 21.5 us: local(): up_act = jnp.dot(rows, w_up[0], preferred_element_type=jnp.float32)]
    all_gather x1 -> x0, blocking collectives: 24 us -> none  [local(): weights = lax.all_gather(weight, ('node', 'local'), axis=0, tiled=True)]
  transfers between devices with their start and end apart: 2 -> 0, of which waited for: 2 -> 0; matrix products, arithmetic and copies ran while one was open for 1% -> 0% of each run, Pallas kernels for 0% -> 0%
where the time goes in v1:
time: 158 us
  Pallas kernels  151 us (96%)
  local copies, waits for them, and re-layouts  4.43 us (3%)
  other arithmetic  2.21 us (1%)
    pallas_call x1, Pallas kernels, ring(): pl.pallas_call(functools.partial(kernel, n, columns), out_shape=jax.Shape...  151 us

profile of v1, /device:TPU:0, one launch (start us, length us, event | category | flops | bytes accessed | tf_op | source)
XLA Modules:
  0.0 157.6 jit_solution(8411724148930872788)
XLA Ops:
  0.0 0.7 convert_reduce_fusion
  0.7 0.7 multiply_divide_fusion
  1.4 0.8 select_reduce_fusion.1
  2.2 0.1 copy.13
  2.3 0.1 copy.12
  2.5 2.0 %concatenate.3.x_hbm = bf16[128,3712]{1,0:T(8,128)(2,1)} concatenate(bf16[128,3584]{1,0:T(8,128)(2,1)} %param.7, bf16[128,64]{1,0:T(8,128)(2,1)S(1)} %pad.9, bf16[128,64]{1,0:T(8,128)(2,1)S(1)} %pad.10), dimensions={1} | concatenate | bytes 1900544 | tf_op jit(solution)/shard_map/concatenate | solution.py:310
  4.5 150.9 %shard_map.73 = bf16[128,3584]{1,0:T(8,128)(2,1)} custom-call(bf16[128,3712]{1,0:T(8,128)(2,1)} %concatenate.3.x_hbm, bf16[3584,1024]{1,0:T(8,128)(2,1)} %bitcast.3, bf16[3584,1024]{1,0:T(8,128)(2,1)} %bitcast.4, bf16[1024,3584]{1,0:T(8,128)(2,1)} %bitcast.5), custom_call_target="tpu_custom_call" | custom-call | flops 45097156608 | bytes 22020096 | tf_op jit(solution)/shard_map/pallas_call | solution.py:316
  155.4 2.2 %copy.16 = bf16[128,3584]{1,0:T(8,128)(2,1)} copy(bf16[128,3584]{1,0:T(8,128)(2,1)} %shard_map.73) | data formatting | bytes 1835008
  (5 shorter events, 0.1 us)

commit v2 on v1

--- a/solution.py
+++ b/solution.py
@@ -44,11 +44,15 @@
     n,
     columns,
     x_hbm,
+    ids_ref,
+    level_ref,
+    where_ref,
     wg_hbm,
     wu_hbm,
     wd_hbm,
     out_ref,
     xbuf,
+    mbuf,
     wg,
     wu,
     wd,
@@ -60,6 +64,10 @@
     load_sem,
     ag_send,
     ag_recv,
+    mk_send,
+    mk_recv,
+    mx_send,
+    mx_recv,
     xs_send,
     xs_recv,
     ys_send,
@@ -69,6 +77,7 @@
 ):
     node = lax.axis_index("node")
     core = lax.axis_index("local")
+    me = node * 2 + core
     K = n // 2
     T = x_hbm.shape[0]
     H = T // 2
@@ -93,7 +102,10 @@
     left = {"node": node_at((pos + n - 1) % n), "local": core}
     other = {"node": node, "local": 1 - core}
 
-    loads = [pltpu.make_async_copy(x_hbm.at[pl.ds(h * H, H)], xbuf.at[pl.ds(h * n * T, H)], load_sem.at[h]) for h in range(2)]
+    loads = []
+    for h in range(2):
+        part, place = pl.ds(h * H, H), pl.ds(h * n * T, H)
+        loads += [pltpu.make_async_copy(x_hbm.at[part], xbuf.at[place], load_sem.at[h])]
     loads += [
         pltpu.make_async_copy(src, dst, load_sem.at[2 + i])
         for i, (src, dst) in enumerate(((wg_hbm, wg), (wu_hbm, wu), (wd_hbm, wd)))
@@ -134,6 +146,62 @@
             device_id_type=MESH,
         )
 
+    E = where_ref.shape[0]
+    B = 2 * E
+
+    def kbase(s):
+        return 0 if s == 0 else 2 * B + (s - 1) * 4 * B
+
+    def mk(d, s):
+        src = kbase(0) if s == 1 else kbase(s - 1) + d * B
+        dst = kbase(s) + (d * B if s < K else 0)
+        i = d * K + s - 1
+        return pltpu.make_async_remote_copy(
+            mbuf.at[pl.ds(src, B)],
+            mbuf.at[pl.ds(dst, B)],
+            mk_send.at[i],
+            mk_recv.at[i],
+            device_id=(right, left)[d],
+            device_id_type=MESH,
+        )
+
+    def mx(s):
+        size = count(s) * B
+        return pltpu.make_async_remote_copy(
+            mbuf.at[pl.ds(kbase(s), size)],
+            mbuf.at[pl.ds(kbase(s) + size, size)],
+            mx_send.at[s],
+            mx_recv.at[s],
+            device_id=other,
+            device_id_type=MESH,
+        )
+
+    def write_marks():
+        levels = level_ref[...].astype(jnp.float32)
+        shares = route_scale * levels / jnp.sum(levels, axis=1, keepdims=True)
+        lanes = lax.broadcasted_iota(jnp.int32, (T, LANES), 1)
+        table = jnp.zeros((T, LANES), jnp.float32)
+        for j in range(ids_ref.shape[1]):
+            table = table + jnp.where(ids_ref[:, j : j + 1] == lanes, shares[:, j : j + 1], 0.0)
+        flipped = table.T[0:E]
+        high = flipped.astype(jnp.bfloat16)
+        mbuf[0:E, :] = high
+        mbuf[E:B, :] = (flipped - high.astype(jnp.float32)).astype(jnp.bfloat16)
+
+    def share_column(h, s):
+        rows = lax.broadcasted_iota(jnp.int32, (B, 1), 0)
+        owner = jnp.zeros((B, 1), jnp.int32)
+        for e in range(E):
+            owner = jnp.where((rows == e) | (rows == e + E), where_ref[e], owner)
+        eye = lax.broadcasted_iota(jnp.int32, (H, T), 0) + h * H
+        eye = eye == lax.broadcasted_iota(jnp.int32, (H, T), 1)
+        parts = []
+        for k in range(2 * count(s)):
+            tile = mbuf[kbase(s) + k * B : kbase(s) + (k + 1) * B, :].astype(jnp.float32)
+            row = jnp.sum(jnp.where(owner == me, tile, 0.0), axis=0, keepdims=True)
+            parts.append(jnp.sum(jnp.where(eye, row, 0.0), axis=1, keepdims=True))
+        return jnp.concatenate(parts, axis=0)
+
     def xs(h, s):
         size = count(s) * H
         i = h * (K + 1) + s
@@ -181,18 +249,24 @@
         return [(d, sub) for sub in range(2) for d in range(2) if s < K or sub == d]
 
     def arrive(h, s):
-        for d, sub in ([(0, 0), (0, 1)] if s == 0 else messages(s)):
-            if s > 0:
+        if s > 0:
+            for d, sub in messages(s):
                 ag(d, h, s, sub).wait_recv()
                 if s < K and (d, sub) in messages(s + 1):
                     ag(d, h, s + 1, sub).start()
-            else:
-                for way, part in messages(1):
-                    if part == sub:
-                        ag(way, h, 1, sub).start()
         xs(h, s).start()
-
-    me = node * 2 + core
+        if h == 0:
+            for d in range(2):
+                if 0 < s and (s < K or d == 0):
+                    mk(d, s).wait_recv()
+                if s < K - 1 or (s == K - 1 and d == 0):
+                    mk(d, s + 1).start()
+            mx(s).start()
+
+    def begin(h, sub):
+        for d in range(2):
+            ag(d, h, 1, sub).start()
+
 
     def compute(h, s):
         size = count(s) * H
@@ -202,17 +276,15 @@
         place = order.index((h, s))
         if place >= 2:
             ys(*order[place - 2]).wait_send()
-        lanes = lax.broadcasted_iota(jnp.int32, (rows, LANES), 1)
-        marks = xbuf[base : base + rows, D : D + LANES].astype(jnp.float32)
-        share = jnp.sum(
-            jnp.where((lanes == me) | (lanes == me + LANES // 2), marks, 0.0), axis=1, keepdims=True
-        )
+        if h == 0:
+            mx(s).wait_recv()
+        share = share_column(h, s)
         wide = 256
 
         @pl.loop(0, F // wide)
         def _(f):
             cols = pl.ds(pl.multiple_of(f * wide, wide), wide)
-            x = xbuf[base : base + rows, 0:D]
+            x = xbuf[base : base + rows, :]
             gate = jnp.dot(x, wg[:, cols], preferred_element_type=jnp.float32)
             up = jnp.dot(x, wu[:, cols], preferred_element_type=jnp.float32)
             hid[0:rows, cols] = (gate / (1.0 + jnp.exp(-gate)) * up).astype(jnp.bfloat16)
@@ -231,7 +303,7 @@
 
     def reduce(h, s):
         ys(h, s).wait_recv()
-        for d, sub in messages(s):
+        for d, sub in messages(s) if s == K else ((0, 1), (1, 0), (0, 0), (1, 1)):
             m = mrow(d, h, s, sub)
             more = s < K and (d, sub) in messages(s + 1)
             if more:
@@ -260,14 +332,21 @@
                 out_ref[o : o + 16, :] = total.astype(jnp.bfloat16)
 
     loads[0].wait()
+    begin(0, 0)
+    write_marks()
     arrive(0, 0)
-    loads[1].wait()
-    for copy in loads[2:]:
+    for copy in loads[1:]:
         copy.wait()
+    for d in range(2):
+        ag(d, 0, 1, 0).wait_send()
+    begin(0, 1)
     for s in range(1, K + 1):
         arrive(0, s)
         if s == K - 1:
+            begin(1, 0)
             arrive(1, 0)
+        if s == K:
+            begin(1, 1)
         compute(0, s - 1)
     arrive(1, 1)
     compute(0, K)
@@ -291,10 +370,17 @@
     for h in range(2):
         for s in range(1, K + 1):
             for d, sub in messages(s):
-                ag(d, h, s, sub).wait_send()
+                if (h, s, sub) != (0, 1, 0):
+                    ag(d, h, s, sub).wait_send()
                 rs(d, h, s, sub).wait_send()
         for s in range(K + 1):
             xs(h, s).wait_send()
+    for s in range(1, K + 1):
+        for d in range(2):
+            if s < K or d == 0:
+                mk(d, s).wait_send()
+    for s in range(K + 1):
+        mx(s).wait_send()
     for item in order[-2:]:
         ys(*item).wait_send()
 
@@ -303,23 +389,20 @@
     T, D = tokens.shape
     F = w_gate.shape[2]
     K = n // 2
-    weight = device_shares(expert_ids, gate_levels, placement)
-    high = lax.reduce_precision(weight, 8, 7)
-    low = weight - high
-    room = ((0, 0), (0, LANES // 2 - placement.shape[0]))
-    rows = jnp.concatenate(
-        [tokens, jnp.pad(high, room).astype(jnp.bfloat16), jnp.pad(low, room).astype(jnp.bfloat16)],
-        axis=1,
-    )
+    E = placement.shape[0]
     bf = jnp.bfloat16
     dma = pltpu.SemaphoreType.DMA
     return pl.pallas_call(
         functools.partial(kernel, n, columns),
         out_shape=jax.ShapeDtypeStruct((T, D), bf),
-        in_specs=[pl.BlockSpec(memory_space=pl.ANY)] * 4,
+        in_specs=[pl.BlockSpec(memory_space=pl.ANY)]
+        + [pl.BlockSpec(memory_space=pltpu.VMEM)] * 2
+        + [pl.BlockSpec(memory_space=pltpu.SMEM)]
+        + [pl.BlockSpec(memory_space=pl.ANY)] * 3,
         out_specs=pl.BlockSpec(memory_space=pltpu.VMEM),
         scratch_shapes=[
-            pltpu.VMEM((2 * n * T, D + LANES), bf),
+            pltpu.VMEM((2 * n * T, D), bf),
+            pltpu.VMEM((4 * n * E, T), bf),
             pltpu.VMEM((D, F), bf),
             pltpu.VMEM((D, F), bf),
             pltpu.VMEM((F, D), bf),
@@ -331,6 +414,10 @@
             dma((5,)),
             dma((8 * K,)),
             dma((8 * K,)),
+            dma((2 * K,)),
+            dma((2 * K,)),
+            dma((K + 1,)),
+            dma((K + 1,)),
             dma((2 * K + 2,)),
             dma((2 * K + 2,)),
             dma((2 * K + 2,)),
@@ -344,7 +431,7 @@
         cost_estimate=pl.CostEstimate(
             flops=12 * n * T * D * F, bytes_accessed=6 * D * F, transcendentals=2 * n * T * F
         ),
-    )(rows, w_gate[0], w_up[0], w_down[0])
+    )(tokens, expert_ids, gate_levels, placement, w_gate[0], w_up[0], w_down[0])
 
 
 def solution(mesh):

time: 158 us -> 158 us (level)
  other arithmetic: 2.21 us -> 0 us
    unnamed x1 -> x3, local copies, waits for them, and re-layouts: 2.16 us -> 4.98 us
    concatenate x1 -> x0, local copies, waits for them, and re-layouts: 2.04 us -> none  [ring(): jnp.concatenate([tokens, jnp.pad(high, room).astype(jnp.bfloat16), jnp.pa...]
where the time goes in v2:
time: 158 us; the launch traced here: 157 us
  Pallas kernels  152 us (96%)
  local copies, waits for them, and re-layouts  4.98 us (3%)
    pallas_call x1, Pallas kernels, ring(): pl.pallas_call(functools.partial(kernel, n, columns), out_shape=jax.Shape...  152 us
    unnamed x3, local copies, waits for them, and re-layouts  4.98 us

profile of v2, /device:TPU:0, one launch (start us, length us, event | category | flops | bytes accessed | tf_op | source)
XLA Modules:
  0.0 157.4 jit_solution(15209601341500973824)
XLA Ops:
  0.0 1.4 copy.8.ids_ref
  1.4 1.4 copy.9.level_ref
  2.8 152.4 %shard_map.73 = bf16[128,3584]{1,0:T(8,128)(2,1)} custom-call(bf16[128,3584]{1,0:T(8,128)(2,1)} %x_hbm.1, s32[128,8]{1,0:T(8,128)} %copy.8.ids_ref, s32[128,8]{1,0:T(8,128)} %copy.9.level_ref, s32[16]{0:T(128)} %where_ref.1, bf16[3584,1024]{1,0:T(8,128)(2,1)} %bitcast.3, bf16[3584,1024]{1,0:T(8,128)(2,1)} %bitcast.4, bf16[1024,3584]{1,0:T(8,128)(2,1)} %bitcast.5), custom_call_target="tpu_custom_call" | custom-call | flops 45097156608 | bytes 22020096 | tf_op jit(solution)/shard_map/pallas_call | solution.py:395
  155.2 2.2 %copy.11 = bf16[128,3584]{1,0:T(8,128)(2,1)} copy(bf16[128,3584]{1,0:T(8,128)(2,1)} %shard_map.73) | data formatting | bytes 1835008
